TPU v7x, 32 devices: a whole 2x2x4 slice. The times are simulated.
32 devices in a mesh: parts: 2 (over x), outer: 2 (over core), inner: 8 (over z, y).
Axes of the slice: x: 2, y: 2, z: 4, core: 2. Of those that a mesh axis runs over, the one named last changes fastest.
Arguments:
- tokens: bfloat16 [2048, 3584], P(('parts', 'outer', 'inner')), parts along dimension 0, may hold values from -6 to 6
- scales: bfloat16 [2048, 28], P(('parts', 'outer', 'inner')), parts along dimension 0, may hold values from 0.5 to 2
- expert_ids: int32 [2048, 8], P(('parts', 'outer', 'inner')), parts along dimension 0, may hold values from 0 to 15, all different within a row; in each aligned block of 64 rows (0 to 63, 64 to 127, ...) at most 64 rows name the same one
- route_weights: float32 [2048, 8], P(('parts', 'outer', 'inner')), parts along dimension 0, may hold values from 0.05 to 0.5
- w_gate: bfloat16 [16, 3584, 1024], P(('outer', 'inner')), may hold values from -0.09375 to 0.09375
- w_up: bfloat16 [16, 3584, 1024], P(('outer', 'inner')), may hold values from -0.09375 to 0.09375
- w_down: bfloat16 [16, 1024, 3584], P(('outer', 'inner')), may hold values from -0.1875 to 0.1875
Outputs:
- mixed: bfloat16 [2048, 3584], P(('parts', 'outer', 'inner')), parts along dimension 0
There are 2 independent parts, one for each index of `parts`. A program takes and returns all parts, laid end to end along the dimension named above; an argument that names none is the same for every part. Nothing has to cross between parts.
Inputs may be any that keep to these rules, and one draw needn't show every extreme that they name: `expert_ids`: each row names 8 different experts; among the rows of one device no expert is named more than 64 times.
All inputs are finite; a program needn't handle non-finite values.
Results may differ from a plain program's by a relative error of at most 0.0071.
Values may be sent and summed in bfloat16 or wider, within the bound.
A program may use at most 128 MiB of HBM per device.

v0:
```python
import jax
import jax.numpy as jnp
from jax import lax
from jax.sharding import PartitionSpec as P


def dequantize(values, block_scales):
    row_count, model_width = values.shape
    scaled = (
        values.astype(jnp.float32).reshape(row_count, model_width // 128, 128)
        * block_scales.astype(jnp.float32)[:, :, None]
    )
    return scaled.reshape(row_count, model_width).astype(jnp.bfloat16)


def expert_ffn(row_block, gate_weight, up_weight, down_weight):
    gate_proj = jnp.dot(row_block, gate_weight, preferred_element_type=jnp.float32)
    up_proj = jnp.dot(row_block, up_weight, preferred_element_type=jnp.float32)
    hidden = (jax.nn.silu(gate_proj) * up_proj).astype(jnp.bfloat16)
    return jnp.dot(hidden, down_weight, preferred_element_type=jnp.float32).astype(jnp.bfloat16)


def route_slots(flat_ids, groups):
    onehot = (flat_ids[:, None] == jnp.arange(groups, dtype=jnp.int32)[None, :]).astype(jnp.int32)
    before = jnp.cumsum(onehot, axis=0) - onehot
    return jnp.sum(before * onehot, axis=1)


def body(tokens, scales, expert_ids, route_weights, w_gate, w_up, w_down):
    outer_n = lax.axis_size("outer")
    inner_n = lax.axis_size("inner")
    groups = outer_n * inner_n
    rows_dev, model_width = tokens.shape
    route_count = expert_ids.shape[1]
    capacity = 2 * rows_dev * route_count // groups
    block_count = scales.shape[1]
    gate_weight, up_weight, down_weight = (w_gate[0], w_up[0], w_down[0])
    source_row = jnp.arange(rows_dev * route_count, dtype=jnp.int32) // route_count
    flat_ids = expert_ids.reshape(-1)
    position = route_slots(flat_ids, groups)
    slot_index = flat_ids * capacity + position
    send_rows = (
        jnp.zeros((groups * capacity, model_width), jnp.bfloat16)
        .at[slot_index]
        .set(tokens[source_row])
    )
    send_scales = (
        jnp.zeros((groups * capacity, block_count), jnp.bfloat16)
        .at[slot_index]
        .set(scales[source_row])
    )
    row_pieces = lax.all_to_all(
        send_rows.reshape(groups, capacity, model_width),
        ("outer", "inner"),
        split_axis=0,
        concat_axis=0,
        tiled=True,
    )
    row_count = row_pieces.shape[0] * row_pieces.shape[1]
    dequant = dequantize(
        row_pieces.reshape(row_count, model_width),
        lax.all_to_all(
            send_scales.reshape(groups, capacity, block_count),
            ("outer", "inner"),
            split_axis=0,
            concat_axis=0,
            tiled=True,
        ).reshape(row_count, block_count),
    )
    result = expert_ffn(dequant, gate_weight, up_weight, down_weight).reshape(row_pieces.shape)
    back = lax.all_to_all(result, ("outer", "inner"), split_axis=0, concat_axis=0, tiled=True)
    collected = (
        back.reshape(groups * capacity, model_width)[slot_index]
        .astype(jnp.float32)
        .reshape(rows_dev, route_count, model_width)
    )
    return jnp.sum(collected * route_weights[:, :, None], axis=1).astype(jnp.bfloat16)


def solution(mesh):
    return jax.shard_map(
        body,
        mesh=mesh,
        in_specs=(
            P(("parts", "outer", "inner"), None),
            P(("parts", "outer", "inner"), None),
            P(("parts", "outer", "inner"), None),
            P(("parts", "outer", "inner"), None),
            P(("outer", "inner"), None, None),
            P(("outer", "inner"), None, None),
            P(("outer", "inner"), None, None),
        ),
        out_specs=P(("parts", "outer", "inner"), None),
        check_vma=False,
    )
```

profile of v0, /device:TPU:8, one launch (start us, length us, event | category | flops | bytes accessed | tf_op | source)
XLA Modules:
  0.0 457.4 jit_solution(12038262890729844296)
XLA Ops:
  0.0 0.8 copy.46
  1.0 0.7 broadcast_multiply_fusion
  1.7 1.2 reduce-window.6
  2.9 0.2 slice_reduce_fusion
  3.3 0.8 copy.49
  4.2 3.1 scatter_custom_fusion.1
  7.3 0.2 copy.51
  7.5 0.8 reshape.205
  8.3 6.8 %all-to-all-start.1 = ((bf16[16,2,896]{2,1,0:T(2,128)(2,1)}), bf16[16,2,896]{2,1,0:T(2,128)(2,1)S(1)}, u32[]{:S(2)}, u32[]{:S(2)}) async-start(bf16[16,2,896]{2,1,0:T(2,128)(2,1)} %reshape.205), calls=%async_computation.1 | async-start | bytes 114688 | tf_op jit(solution)/shard_map/all_to_all | solution.py:62
  15.1 20.7 %scatter_custom_fusion = bf16[1024,3584]{1,0:T(8,128)(2,1)} fusion(s32[512]{0:T(512)S(1)} %bitcast.56, bf16[64,3584]{1,0:T(8,128)(2,1)S(1)} %copy-done, s32[1024]{0:T(1024)S(1)} %pad_clamp_fusion.1, bf16[]{:T(256)} %constant.26.clone.1), kind=kCustom, calls=%fused_computation.15 | custom fusion | bytes 7340034 | tf_op jit(solution)/shard_map/scatter | solution.py:45
  35.8 6.4 %all-to-all-start = ((bf16[16,64,3584]{2,1,0:T(8,128)(2,1)}), bf16[16,64,3584]{2,1,0:T(8,128)(2,1)}, u32[]{:S(2)}, u32[]{:S(2)}) async-start(bf16[16,64,3584]{2,1,0:T(8,128)(2,1)} %bitcast.47), calls=%async_computation | async-start | bytes 14680064 | tf_op jit(solution)/shard_map/all_to_all | solution.py:52
  42.2 0.1 reshape.206
  42.4 0.2 copy.58
  42.6 160.4 %all-to-all-done = bf16[16,64,3584]{2,1,0:T(8,128)(2,1)} async-done(((bf16[16,64,3584]{2,1,0:T(8,128)(2,1)}), bf16[16,64,3584]{2,1,0:T(8,128)(2,1)}, u32[]{:S(2)}, u32[]{:S(2)}) %all-to-all-start) | async-done | bytes 7340064 | tf_op jit(solution)/shard_map/all_to_all | solution.py:52
  203.0 13.6 %reshape.149 = f32[1024,28,128]{2,1,0:T(8,128)} reshape(bf16[16,64,3584]{2,1,0:T(8,128)(2,1)} %all-to-all-done) | data formatting | bytes 22020096 | tf_op jit(solution)/shard_map/convert_element_type | solution.py:10
  216.7 12.7 %multiply_convert_fusion = bf16[1024,28,128]{2,1,0:T(8,128)(2,1)} fusion(f32[1024,28,128]{2,1,0:T(8,128)} %reshape.149, f32[1024,28]{1,0:T(8,128)S(1)} %bitcast.51), kind=kLoop, calls=%fused_computation.5 | loop fusion | flops 7340032 | bytes 22134784 | tf_op jit(solution)/shard_map/convert_element_type | solution.py:13
  229.3 12.0 %copy.54 = bf16[1024,28,128]{0,2,1:T(8,128)(2,1)} copy(bf16[1024,28,128]{2,1,0:T(8,128)(2,1)} %multiply_convert_fusion) | data formatting | bytes 14680064 | tf_op jit(solution)/shard_map/convert_element_type | solution.py:13
  241.3 11.8 %fusion.2 = f32[1024,1024]{1,0:T(8,128)S(1)} fusion(bf16[1024,3584]{0,1:T(8,128)(2,1)} %bitcast.49, bf16[1,3584,1024]{2,1,0:T(8,128)(2,1)} %param.12), kind=kOutput, calls=%fused_computation.10 | convolution fusion | flops 7516192768 | bytes 18874368 | tf_op jit(solution)/shard_map/dot_general | solution.py:18
  253.1 10.9 %multiply_convert_fusion.1 = bf16[1024,1024]{1,0:T(8,128)(2,1)S(1)} fusion(f32[1024,1024]{1,0:T(8,128)S(1)} %fusion.2, bf16[1024,3584]{0,1:T(8,128)(2,1)S(1)} %bitcast.50, bf16[1,3584,1024]{2,1,0:T(8,128)(2,1)} %param.11), kind=kOutput, calls=%fused_computation.14 | convolution fusion | flops 7522484224 | bytes 20971520 | tf_op jit(solution)/shard_map/dot_general | solution.py:17
  264.0 9.8 %convolution_convert_fusion = bf16[1024,3584]{1,0:T(8,128)(2,1)} fusion(bf16[1024,1024]{1,0:T(8,128)(2,1)S(1)} %multiply_convert_fusion.1, bf16[1,1024,3584]{2,1,0:T(8,128)(2,1)S(1)} %bitcast.61), kind=kOutput, calls=%fused_computation.6 | convolution fusion | flops 7519862784 | bytes 16777216 | tf_op jit(solution)/shard_map/dot_general | solution.py:20
  273.9 5.0 %all-to-all-start.2 = ((bf16[16,64,3584]{2,1,0:T(8,128)(2,1)}), bf16[16,64,3584]{2,1,0:T(8,128)(2,1)}, u32[]{:S(2)}, u32[]{:S(2)}) async-start(bf16[16,64,3584]{2,1,0:T(8,128)(2,1)} %bitcast.48), calls=%async_computation.2 | async-start | bytes 14680064 | tf_op jit(solution)/shard_map/all_to_all | solution.py:71
  278.9 160.4 %all-to-all-done.2 = bf16[16,64,3584]{2,1,0:T(8,128)(2,1)} async-done(((bf16[16,64,3584]{2,1,0:T(8,128)(2,1)}), bf16[16,64,3584]{2,1,0:T(8,128)(2,1)}, u32[]{:S(2)}, u32[]{:S(2)}) %all-to-all-start.2) | async-done | bytes 7340064 | tf_op jit(solution)/shard_map/all_to_all | solution.py:71
  439.3 12.0 %gather_fusion = bf16[512,3584]{1,0:T(8,128)(2,1)} fusion(bf16[1024,3584]{1,0:T(8,128)(2,1)} %bitcast.12, s32[1024]{0:T(1024)S(1)} %pad_clamp_fusion), kind=kCustom, calls=%fused_computation.2 | custom fusion | bytes 7342080 | tf_op jit(solution)/shard_map/gather | solution.py:73
  451.3 5.8 %fusion = bf16[64,3584]{1,0:T(8,128)(2,1)} fusion(bf16[512,3584]{1,0:T(8,128)(2,1)} %gather_fusion, f32[64,8]{1,0:T(8,128)S(1)} %copy.55), kind=kLoop, calls=%fused_computation.8 | loop fusion | flops 5275648 | bytes 4130816 | tf_op jit(solution)/shard_map/reduce_sum | solution.py:77
  (28 shorter events, 0.7 us)
Async XLA Ops:
  0.0 15.1 %copy-start = (bf16[64,3584]{1,0:T(8,128)(2,1)S(1)}, bf16[64,3584]{1,0:T(8,128)(2,1)}, u32[]{:S(2)}) copy-start(bf16[64,3584]{1,0:T(8,128)(2,1)} %param.7) | copy-start | bytes 1376260
  8.3 27.5 %all-to-all-start.1 = ((bf16[16,2,896]{2,1,0:T(2,128)(2,1)}), bf16[16,2,896]{2,1,0:T(2,128)(2,1)S(1)}, u32[]{:S(2)}, u32[]{:S(2)}) async-start(bf16[16,2,896]{2,1,0:T(2,128)(2,1)} %reshape.205), calls=%async_computation.1 | async-start | bytes 114688 | tf_op jit(solution)/shard_map/all_to_all | solution.py:62
  35.8 167.3 %all-to-all-start = ((bf16[16,64,3584]{2,1,0:T(8,128)(2,1)}), bf16[16,64,3584]{2,1,0:T(8,128)(2,1)}, u32[]{:S(2)}, u32[]{:S(2)}) async-start(bf16[16,64,3584]{2,1,0:T(8,128)(2,1)} %bitcast.47), calls=%async_computation | async-start | bytes 14680064 | tf_op jit(solution)/shard_map/all_to_all | solution.py:52
  241.3 11.8 %copy-start.2 = (bf16[1024,28,128]{0,2,1:T(8,128)(2,1)S(1)}, bf16[1024,28,128]{0,2,1:T(8,128)(2,1)}, u32[]{:S(2)}) copy-start(bf16[1024,28,128]{0,2,1:T(8,128)(2,1)} %copy.54) | copy-start | bytes 22020100
  241.3 22.7 %slice-start = ((s8[7340032]{0:T(1024)(128)(4,1)}), s8[4194304]{0:T(1024)(128)(4,1)S(1)}, s32[]{:S(2)}) async-start(s8[7340032]{0:T(1024)(128)(4,1)} %bitcast.60), calls=%async_computation.3 | async-start | bytes 8388608
  253.1 11.0 %slice-start.1 = ((s8[7340032]{0:T(1024)(128)(4,1)}), s8[3145728]{0:T(1024)(128)(4,1)S(1)}, s32[]{:S(2)}) async-start(s8[7340032]{0:T(1024)(128)(4,1)} %bitcast.60), calls=%async_computation.4 | async-start | bytes 6291456
  273.8 5.0 %copy-start.3 = (f32[64,8]{0,1:T(8,128)S(1)}, f32[64,8]{0,1:T(8,128)}, u32[]{:S(2)}) copy-start(f32[64,8]{0,1:T(8,128)} %param.10) | copy-start | bytes 6148
  273.9 165.4 %all-to-all-start.2 = ((bf16[16,64,3584]{2,1,0:T(8,128)(2,1)}), bf16[16,64,3584]{2,1,0:T(8,128)(2,1)}, u32[]{:S(2)}, u32[]{:S(2)}) async-start(bf16[16,64,3584]{2,1,0:T(8,128)(2,1)} %bitcast.48), calls=%async_computation.2 | async-start | bytes 14680064 | tf_op jit(solution)/shard_map/all_to_all | solution.py:71
  439.3 17.8 %copy-start.1 = (bf16[64,3584]{1,0:T(8,128)(2,1)S(1)}, bf16[64,3584]{1,0:T(8,128)(2,1)}, u32[]{:S(2)}) copy-start(bf16[64,3584]{1,0:T(8,128)(2,1)} %param.7) | copy-start | bytes 1376260
where the time goes:
time: 462 us; the launch traced here: 457 us
  waiting for transfers between devices  321 us (69%)
  local copies, waits for them, and re-layouts  65 us (14%)
  matrix products  32.5 us (7%)
  other arithmetic  20.5 us (4%)
  starting transfers between devices  18.1 us (4%)
    all_to_all x1, waiting for transfers between devices, body(): lax.all_to_all(send_rows.reshape(groups, capacity, model_width), ('outer'...  160 us
    all_to_all x1, waiting for transfers between devices, body(): lax.all_to_all(result, ('outer', 'inner'), split_axis=0, concat_axis=0, t...  160 us
    scatter x1, local copies, waits for them, and re-layouts, body(): send_rows = jnp.zeros((groups * capacity, model_width), jnp.bfloat16).at[...  20.7 us
    convert_element_type x1, local copies, waits for them, and re-layouts, dequantize(): values.astype(jnp.float32).reshape(row_count, model_width // 128, 128)  13.6 us
    convert_element_type x1, other arithmetic, dequantize(): return scaled.reshape(row_count, model_width).astype(jnp.bfloat16)  12.7 us
    gather x1, local copies, waits for them, and re-layouts, body(): back.reshape(groups * capacity, model_width)[slot_index].astype(jnp.float32)  12 us
    convert_element_type x1, local copies, waits for them, and re-layouts, dequantize(): return scaled.reshape(row_count, model_width).astype(jnp.bfloat16)  12 us
    dot_general x1, matrix products, expert_ffn(): up_proj = jnp.dot(row_block, up_weight, preferred_element_type=jnp.float32)  11.8 us
  transfers between devices with their start and end apart: 3, of which 2 were waited for; matrix products, arithmetic and copies ran while one was open for 5% of the time, Pallas kernels for 0%

commit v1 on v0

v1 whole, which is shorter than its diff:
```python
import jax
import jax.numpy as jnp
from jax import lax
from jax.sharding import PartitionSpec as P

GROUP = ("outer", "inner")


def dequantize(values, block_scales):
    row_count, model_width = values.shape
    scaled = (
        values.astype(jnp.float32).reshape(row_count, model_width // 128, 128)
        * block_scales.astype(jnp.float32)[:, :, None]
    )
    return scaled.reshape(row_count, model_width).astype(jnp.bfloat16)


def body(tokens, scales, expert_ids, route_weights, w_gate, w_up, w_down):
    groups = lax.axis_size("outer") * lax.axis_size("inner")
    me = lax.axis_index("outer") * lax.axis_size("inner") + lax.axis_index("inner")
    experts = jnp.arange(groups, dtype=jnp.int32)
    dense = jnp.sum(
        jnp.where(expert_ids[:, :, None] == experts, route_weights[:, :, None], 0.0), axis=1
    )
    mine = lax.all_gather(dense, GROUP, axis=0, tiled=True)
    weight = lax.dynamic_slice_in_dim(mine, me, 1, axis=1)
    rows = lax.all_gather(dequantize(tokens, scales), GROUP, axis=0, tiled=True)
    gate = jnp.dot(rows, w_gate[0], preferred_element_type=jnp.float32)
    up = jnp.dot(rows, w_up[0], preferred_element_type=jnp.float32)
    hidden = (jax.nn.silu(gate) * up).astype(jnp.bfloat16)
    out = jnp.dot(hidden, w_down[0], preferred_element_type=jnp.float32)
    out = (out * weight).astype(jnp.bfloat16)
    return lax.psum_scatter(out, GROUP, scatter_dimension=0, tiled=True)


def solution(mesh):
    rows = P(("parts", "outer", "inner"), None)
    weights = P(("outer", "inner"), None, None)
    return jax.shard_map(
        body,
        mesh=mesh,
        in_specs=(rows, rows, rows, rows, weights, weights, weights),
        out_specs=rows,
        check_vma=False,
    )
```

time: 462 us -> 211 us (0.46)
  the two profiles are of different devices: /device:TPU:8 before, /device:TPU:0 now
where the time goes in v1:
time: 211 us
  waiting for transfers between devices  126 us (60%)
  blocking collectives  35.7 us (17%)
  matrix products  32 us (15%)
  between operations  13.5 us (6%)
  other arithmetic  3.03 us (1%)
    reduce_scatter x1, waiting for transfers between devices, body(): return lax.psum_scatter(out, GROUP, scatter_dimension=0, tiled=True)  90.3 us
    all_gather x1, blocking collectives, body(): mine = lax.all_gather(dense, GROUP, axis=0, tiled=True)  35.7 us
    all_gather x1, waiting for transfers between devices, body(): rows = lax.all_gather(dequantize(tokens, scales), GROUP, axis=0, tiled=True)  35.3 us
    dot_general x1, matrix products, body(): up = jnp.dot(rows, w_up[0], preferred_element_type=jnp.float32)  11.4 us
    dot_general x1, matrix products, body(): gate = jnp.dot(rows, w_gate[0], preferred_element_type=jnp.float32)  10.8 us
    dot_general x1, matrix products, body(): out = jnp.dot(hidden, w_down[0], preferred_element_type=jnp.float32)  9.86 us
  transfers between devices with their start and end apart: 2, of which 2 were waited for; matrix products, arithmetic and copies ran while one was open for 0% of the time, Pallas kernels for 0%

profile of v1, /device:TPU:0, one launch (start us, length us, event | category | flops | bytes accessed | tf_op | source)
XLA Modules:
  0.0 211.1 jit_solution(14173992496145467530)
XLA Ops:
  6.5 0.0 all-gather.3.cloned.1.call-start
  6.5 0.8 copy.21
  7.3 0.3 mul.31
  7.7 2.3 %fusion.7 = bf16[64,3584]{1,0:T(8,128)(2,1)} fusion(f32[8,8,28,128]{3,2,1,0:T(8,128)S(1)} %bitcast.23, bf16[64,3584]{1,0:T(8,128)(2,1)} %param.7), kind=kLoop, calls=%fused_computation.8 | loop fusion | flops 688128 | bytes 1835008 | tf_op jit(solution)/shard_map/convert_element_type | solution.py:15
  10.0 0.0 all-gather.3.cloned.1.call-update
  10.0 0.0 reduce-scatter.2.cloned.1.call-start
  10.0 0.7 select_reduce_fusion
  10.8 35.7 %all-gather = f32[16,64,16]{1,2,0:T(8,128)S(1)} all-gather(f32[1,64,16]{1,2,0:T(8,128)S(1)} %bitcast.24), channel_id=1, replica_groups=mesh['parts'=2,'outer'=2,'inner'=8] {'outer','inner'}, dimensions={0}, use_global_device_ids=true | all-gather | bytes 69632 | tf_op jit(solution)/shard_map/all_gather | solution.py:25
  46.5 0.1 reshape.7
  46.6 35.3 %all-gather.3.cloned.1.call-done = bf16[1024,3584]{1,0:T(8,128)(2,1)} async-done(((bf16[64,3584]{1,0:T(8,128)(2,1)}), bf16[1024,3584]{1,0:T(8,128)(2,1)}) %all-gather.3.cloned.1.call-update) | async-done | bytes 7340048 | tf_op jit(solution)/shard_map/all_gather | solution.py:27
  81.9 0.0 copy-start
  81.9 0.0 slice-start
  81.9 11.4 %fusion.1 = f32[1024,1024]{1,0:T(8,128)S(1)} fusion(bf16[1024,3584]{1,0:T(8,128)(2,1)} %all-gather.3.cloned.1.call-done, bf16[1,3584,1024]{2,1,0:T(8,128)(2,1)} %param.12), kind=kOutput, calls=%fused_computation.2 | convolution fusion | flops 7516192768 | bytes 18874368 | tf_op jit(solution)/shard_map/dot_general | solution.py:29
  93.3 0.0 copy-done
  93.3 0.0 slice-start.1
  93.3 10.8 %multiply_convert_fusion.1 = bf16[1024,1024]{1,0:T(8,128)(2,1)S(1)} fusion(f32[1024,1024]{1,0:T(8,128)S(1)} %fusion.1, bf16[1024,3584]{1,0:T(8,128)(2,1)S(1)} %copy-done, bf16[1,3584,1024]{2,1,0:T(8,128)(2,1)} %param.11), kind=kOutput, calls=%fused_computation.6 | convolution fusion | flops 7522484224 | bytes 20971520 | tf_op jit(solution)/shard_map/dot_general | solution.py:28
  104.1 0.0 slice-done
  104.1 0.0 slice-done.1
  104.1 9.9 %multiply_convert_fusion = bf16[1024,3584]{1,0:T(8,128)(2,1)} fusion(bf16[1024,1024]{1,0:T(8,128)(2,1)S(1)} %multiply_convert_fusion.1, bf16[1,1024,3584]{2,1,0:T(8,128)(2,1)S(1)} %bitcast.27, f32[1024]{0:T(1024)S(1)} %bitcast.25), kind=kOutput, calls=%fused_computation | convolution fusion | flops 7523532800 | bytes 16781312 | tf_op jit(solution)/shard_map/dot_general | solution.py:31
  114.0 0.0 reduce-scatter.2.cloned.1.call-update
  114.0 90.3 %reduce-scatter.2.cloned.1.call-done = bf16[64,3584]{1,0:T(8,128)(2,1)} async-done(((bf16[1024,3584]{1,0:T(8,128)(2,1)}), bf16[64,3584]{1,0:T(8,128)(2,1)}) %reduce-scatter.2.cloned.1.call-update) | async-done | bytes 458768 | tf_op jit(solution)/shard_map/reduce_scatter | solution.py:33
  (3 shorter events, 0.1 us)
Async XLA Ops:
  6.5 75.4 %all-gather.3.cloned.1.call-start = ((), (), s32[]{:S(2)}) async-start(), calls=%async_computation.1 | async-start | bytes 7798784 | tf_op jit(solution)/shard_map/all_gather | solution.py:27
  10.0 194.3 %reduce-scatter.2.cloned.1.call-start = ((), (), s32[]{:S(2)}) async-start(), calls=%async_computation.2 | async-start | bytes 7798784 | tf_op jit(solution)/shard_map/reduce_scatter | solution.py:33
  81.9 11.4 %copy-start = (bf16[1024,3584]{1,0:T(8,128)(2,1)S(1)}, bf16[1024,3584]{1,0:T(8,128)(2,1)}, u32[]{:S(2)}) copy-start(bf16[1024,3584]{1,0:T(8,128)(2,1)} %all-gather.3.cloned.1.call-done) | copy-start | bytes 22020100
  81.9 22.2 %slice-start = ((s8[7340032]{0:T(1024)(128)(4,1)}), s8[4194304]{0:T(1024)(128)(4,1)S(1)}, s32[]{:S(2)}) async-start(s8[7340032]{0:T(1024)(128)(4,1)} %bitcast.26), calls=%async_computation.3 | async-start | bytes 8388608
  93.3 10.8 %slice-start.1 = ((s8[7340032]{0:T(1024)(128)(4,1)}), s8[3145728]{0:T(1024)(128)(4,1)S(1)}, s32[]{:S(2)}) async-start(s8[7340032]{0:T(1024)(128)(4,1)} %bitcast.26), calls=%async_computation.4 | async-start | bytes 6291456
Sparse Core Ops, SparseCore 0:
  10.1 71.7 all-gather.2
  114.1 90.1 reduce-scatter.1

commit v2 on v1

v2 whole, which is shorter than its diff:
```python
import functools

import jax
import jax.numpy as jnp
from jax import lax
from jax.experimental import pallas as pl
from jax.experimental.pallas import tpu as pltpu
from jax.sharding import PartitionSpec as P

LANES = 128
TILE = 256
MESH = pl.DeviceIdType.MESH


def ring_position(chips, index):
    if chips > 8:
        return index
    z, y = index // 2, index % 2
    return z + y * (chips - 1 - 2 * z)


def ring_index(chips, position):
    if chips > 8:
        return position
    back = position // (chips // 2)
    return (1 - back) * 2 * position + back * (2 * (chips - 1 - position) + 1)


def kernel(
    chips, experts,
    tokens, scales, ids, weights, gate_hbm, up_hbm, down_hbm,
    out,
    wg, wu, wd, rows, hidden, own, first, part_out, part_in, sums,
    w_sem, tok_send, tok_recv, swap_send, swap_recv, part_send, part_recv, sum_send, sum_recv,
):
    core = lax.axis_index("outer")
    index = lax.axis_index("inner")
    me = core * chips + index
    position = ring_position(chips, index)
    right = {"inner": ring_index(chips, (position + 1) % chips)}
    left = {"inner": ring_index(chips, (position + chips - 1) % chips)}
    twin = {"outer": 1 - core}
    count, width = tokens.shape
    half = count // 2
    tiles = width // TILE
    ways = ((0, right), (1, left))

    loads = [
        pltpu.make_async_copy(gate_hbm.at[0], wg, w_sem.at[0]),
        pltpu.make_async_copy(up_hbm.at[0], wu, w_sem.at[1]),
        pltpu.make_async_copy(down_hbm.at[0], wd, w_sem.at[2]),
    ]
    for load in loads:
        load.start()

    barrier = pltpu.get_barrier_semaphore()
    for other in (right, left, twin):
        pl.semaphore_signal(barrier, inc=1, device_id=other, device_id_type=MESH)

    for block in range(width // LANES):
        columns = slice(block * LANES, (block + 1) * LANES)
        scaled = tokens[:, columns].astype(jnp.float32) * scales[:, block:block + 1].astype(jnp.float32)
        rows[0, :count, columns] = scaled.astype(jnp.bfloat16)
    lane = lax.broadcasted_iota(jnp.int32, (count, LANES), 1)
    dense = jnp.zeros((count, LANES), jnp.float32)
    for route in range(ids.shape[1]):
        dense = dense + jnp.where(ids[:, route:route + 1] == lane % experts, weights[:, route:route + 1], 0.0)
    high = dense.astype(jnp.bfloat16).astype(jnp.float32)
    middle = (dense - high).astype(jnp.bfloat16).astype(jnp.float32)
    low = dense - high - middle
    piece = lane // experts
    packed = jnp.where(piece == 0, high, jnp.where(piece == 1, middle, jnp.where(piece == 2, low, 0.0)))
    rows[0, :count, width:] = packed.astype(jnp.bfloat16)
    sums[0] = jnp.zeros((count, width), jnp.bfloat16)

    def token_copy(step, way, target):
        part = pl.ds(way * half, half)
        return pltpu.make_async_remote_copy(
            src_ref=rows.at[step, part], dst_ref=rows.at[step + 1, part],
            send_sem=tok_send.at[step, way], recv_sem=tok_recv.at[step + 1, way],
            device_id=target, device_id_type=MESH,
        )

    def swap_copy(step):
        return pltpu.make_async_remote_copy(
            src_ref=rows.at[step, pl.ds(0, count)], dst_ref=rows.at[step, pl.ds(count, count)],
            send_sem=swap_send.at[step], recv_sem=swap_recv.at[step],
            device_id=twin, device_id_type=MESH,
        )

    def part_copy(step):
        return pltpu.make_async_remote_copy(
            src_ref=part_out.at[step % 2], dst_ref=part_in.at[step],
            send_sem=part_send.at[step], recv_sem=part_recv.at[step],
            device_id=twin, device_id_type=MESH,
        )

    def sum_copy(step, way, target):
        part = pl.ds(way * half, half)
        return pltpu.make_async_remote_copy(
            src_ref=sums.at[step - 1, part], dst_ref=sums.at[step, part],
            send_sem=sum_send.at[step - 1, way], recv_sem=sum_recv.at[step, way],
            device_id=target, device_id_type=MESH,
        )

    def pass_on(step):
        @pl.when(step > 0)
        def _():
            for way, target in ways:
                token_copy(step - 1, way, target).wait_recv()

        @pl.when(step < chips - 1)
        def _():
            for way, target in ways:
                token_copy(step, way, target).start()

        swap_copy(step).start()

    def ffn(step):
        def up_tile(tile, carry):
            columns = pl.ds(pl.multiple_of(tile * TILE, TILE), TILE)
            block = rows[step, :, :width]
            gate = jnp.dot(block, wg[:, columns], preferred_element_type=jnp.float32)
            up = jnp.dot(block, wu[:, columns], preferred_element_type=jnp.float32)
            hidden[:, columns] = (gate / (1.0 + jnp.exp(-gate)) * up).astype(jnp.bfloat16)
            return carry

        lax.fori_loop(0, hidden.shape[1] // TILE, up_tile, 0)
        lane = lax.broadcasted_iota(jnp.int32, (2 * count, LANES), 1)
        packed = rows[step, :, width:].astype(jnp.float32)
        share = jnp.sum(jnp.where(lane % experts == me, packed, 0.0), axis=1, keepdims=True)

        def down_tile(tile, carry):
            columns = pl.ds(pl.multiple_of(tile * TILE, TILE), TILE)
            result = jnp.dot(hidden[...], wd[:, columns], preferred_element_type=jnp.float32) * share
            own[:, columns] = result[:count]
            part_out[step % 2, :, columns] = result[count:].astype(jnp.bfloat16)
            return carry

        lax.fori_loop(0, tiles, down_tile, 0)

    pl.semaphore_wait(barrier, 3)
    pass_on(0)
    swap_copy(0).wait_recv()
    for load in loads:
        load.wait()
    ffn(0)
    part_copy(0).start()
    pass_on(1)
    part_copy(0).wait_recv()

    def keep_tile(tile, carry):
        columns = pl.ds(pl.multiple_of(tile * TILE, TILE), TILE)
        first[:, columns] = own[:, columns] + part_in[0, :, columns].astype(jnp.float32)
        return carry

    lax.fori_loop(0, tiles, keep_tile, 0)

    def send_sums(step):
        part_copy(step).wait_recv()

        @pl.when(step > 1)
        def _():
            for way, target in ways:
                sum_copy(step - 1, way, target).wait_recv()

        def add_tile(tile, carry):
            columns = pl.ds(pl.multiple_of(tile * TILE, TILE), TILE)
            total = own[:, columns] + part_in[step, :, columns].astype(jnp.float32)
            total = total + sums[step - 1, :, columns].astype(jnp.float32)
            sums[step - 1, :, columns] = total.astype(jnp.bfloat16)
            return carry

        lax.fori_loop(0, tiles, add_tile, 0)
        for way, target in ways:
            sum_copy(step, way, target).start()

    def turn(step, carry):
        swap_copy(step).wait_recv()

        @pl.when(step > 1)
        def _():
            part_copy(step - 2).wait_send()

        ffn(step)
        part_copy(step).start()

        @pl.when(step < chips - 1)
        def _():
            pass_on(step + 1)

        send_sums(step)
        return carry

    lax.fori_loop(1, chips, turn, 0)
    for way, target in ways:
        sum_copy(chips - 1, way, target).wait_recv()

    def last_tile(tile, carry):
        columns = pl.ds(pl.multiple_of(tile * TILE, TILE), TILE)
        total = first[:, columns] + sums[chips - 1, :, columns].astype(jnp.float32)
        out[:, columns] = total.astype(jnp.bfloat16)
        return carry

    lax.fori_loop(0, tiles, last_tile, 0)
    part_copy(chips - 1).wait_send()
    part_copy(chips - 2).wait_send()

    def drain(step, carry):
        for way, target in ways:
            token_copy(step, way, target).wait_send()
            sum_copy(step + 1, way, target).wait_send()
        return carry

    lax.fori_loop(0, chips - 1, drain, 0)

    def drain_swaps(step, carry):
        swap_copy(step).wait_send()
        return carry

    lax.fori_loop(0, chips, drain_swaps, 0)


def body(tokens, scales, expert_ids, route_weights, w_gate, w_up, w_down):
    chips = lax.axis_size("inner")
    experts = lax.axis_size("outer") * chips
    count, width = tokens.shape
    ff = w_gate.shape[2]
    vmem = pl.BlockSpec(memory_space=pltpu.VMEM)
    hbm = pl.BlockSpec(memory_space=pl.ANY)
    dma = pltpu.SemaphoreType.DMA
    flops = 12 * chips * count * width * ff
    return pl.pallas_call(
        functools.partial(kernel, chips, experts),
        out_shape=jax.ShapeDtypeStruct((count, width), jnp.bfloat16),
        in_specs=[vmem] * 4 + [hbm] * 3,
        out_specs=vmem,
        scratch_shapes=[
            pltpu.VMEM((width, ff), jnp.bfloat16),
            pltpu.VMEM((width, ff), jnp.bfloat16),
            pltpu.VMEM((ff, width), jnp.bfloat16),
            pltpu.VMEM((chips, 2 * count, width + LANES), jnp.bfloat16),
            pltpu.VMEM((2 * count, ff), jnp.bfloat16),
            pltpu.VMEM((count, width), jnp.float32),
            pltpu.VMEM((count, width), jnp.float32),
            pltpu.VMEM((2, count, width), jnp.bfloat16),
            pltpu.VMEM((chips, count, width), jnp.bfloat16),
            pltpu.VMEM((chips, count, width), jnp.bfloat16),
            dma((3,)),
            dma((chips, 2)), dma((chips, 2)),
            dma((chips,)), dma((chips,)),
            dma((chips,)), dma((chips,)),
            dma((chips, 2)), dma((chips, 2)),
        ],
        cost_estimate=pl.CostEstimate(
            flops=flops, bytes_accessed=6 * width * ff, transcendentals=2 * chips * count * ff
        ),
        compiler_params=pltpu.CompilerParams(
            collective_id=0, has_side_effects=True, vmem_limit_bytes=60 * 1024 * 1024
        ),
    )(tokens, scales, expert_ids, route_weights, w_gate, w_up, w_down)


def solution(mesh):
    rows = P(("parts", "outer", "inner"), None)
    weights = P(("outer", "inner"), None, None)
    return jax.shard_map(
        body,
        mesh=mesh,
        in_specs=(rows, rows, rows, rows, weights, weights, weights),
        out_specs=rows,
        check_vma=False,
    )
```

time: 211 us -> 102 us (0.48)
  waiting for transfers between devices: 126 us -> 0 us
  Pallas kernels: 0 us -> 95.3 us
  blocking collectives: 35.7 us -> 0 us
  matrix products: 32 us -> 0 us
  between operations: 13.5 us -> 0.01 us
  local copies, waits for them, and re-layouts: 1.28 us -> 5.95 us
  other arithmetic: 3.03 us -> 0 us
    pallas_call x0 -> x1, Pallas kernels: none -> 95.3 us  [body(): pl.pallas_call(functools.partial(kernel, chips, experts), out_shape=jax.S...]
    reduce_scatter x1 -> x0, waiting for transfers between devices: 90.3 us -> none  [body(): return lax.psum_scatter(out, GROUP, scatter_dimension=0, tiled=True)]
    all_gather x1 -> x0, blocking collectives: 35.7 us -> none  [body(): mine = lax.all_gather(dense, GROUP, axis=0, tiled=True)]
    all_gather x1 -> x0, waiting for transfers between devices: 35.3 us -> none  [body(): rows = lax.all_gather(dequantize(tokens, scales), GROUP, axis=0, tiled=True)]
    dot_general x3 -> x0, matrix products: 32 us -> none  [the longest x1 11.4 us: body(): up = jnp.dot(rows, w_up[0], preferred_element_type=jnp.float32)]
    unnamed x7 -> x4, local copies, waits for them, and re-layouts: 0.11 us -> 5.95 us
    convert_element_type x1 -> x0, other arithmetic: 2.31 us -> none  [dequantize(): return scaled.reshape(row_count, model_width).astype(jnp.bfloat16)]
  transfers between devices with their start and end apart: 2 -> 0, of which waited for: 2 -> 0; matrix products, arithmetic and copies ran while one was open for 0% -> 0% of each run, Pallas kernels for 0% -> 0%
where the time goes in v2:
time: 102 us; the launch traced here: 101 us
  Pallas kernels  95.3 us (93%)
  local copies, waits for them, and re-layouts  5.95 us (6%)
    pallas_call x1, Pallas kernels, body(): pl.pallas_call(functools.partial(kernel, chips, experts), out_shape=jax.S...  95.3 us
    unnamed x4, local copies, waits for them, and re-layouts  5.95 us

profile of v2, /device:TPU:0, one launch (start us, length us, event | category | flops | bytes accessed | tf_op | source)
XLA Modules:
  0.0 101.3 jit_solution(8529208818480140410)
XLA Ops:
  0.0 1.4 %copy.8.scales = bf16[64,28]{1,0:T(8,128)(2,1)} copy(bf16[64,28]{0,1:T(8,128)(2,1)} %param.8) | data formatting | bytes 7168 | tf_op args[1]
  1.4 1.4 %copy.9.ids = s32[64,8]{1,0:T(8,128)} copy(s32[64,8]{0,1:T(8,128)} %param.9) | data formatting | bytes 4096 | tf_op args[2]
  2.8 1.4 %copy.10.weights = f32[64,8]{1,0:T(8,128)} copy(f32[64,8]{0,1:T(8,128)} %param.10) | data formatting | bytes 4096 | tf_op args[3]
  4.1 95.3 %shard_map.73 = bf16[64,3584]{1,0:T(8,128)(2,1)} custom-call(bf16[64,3584]{1,0:T(8,128)(2,1)} %tokens.1, bf16[64,28]{1,0:T(8,128)(2,1)} %copy.8.scales, s32[64,8]{1,0:T(8,128)} %copy.9.ids, f32[64,8]{1,0:T(8,128)} %copy.10.weights, bf16[1,3584,1024]{2,1,0:T(8,128)(2,1)} %gate_hbm.1, bf16[1,3584,1024]{2,1,0:T(8,128)(2,1)} %up_hbm.1, ...), custom_call_target="tpu_custom_call" | custom-call | flops 22548578304 | bytes 22020096 | tf_op jit(solution)/shard_map/pallas_call | solution.py:233
  99.5 1.8 %copy.12 = bf16[64,3584]{1,0:T(8,128)(2,1)} copy(bf16[64,3584]{1,0:T(8,128)(2,1)} %shard_map.73) | data formatting | bytes 917504

commit v3 on v2

--- a/solution.py
+++ b/solution.py
@@ -9,6 +9,7 @@
 
 LANES = 128
 TILE = 256
+PIECES = 2
 MESH = pl.DeviceIdType.MESH
 
 
@@ -43,6 +44,7 @@
     count, width = tokens.shape
     half = count // 2
     tiles = width // TILE
+    chunk = width // PIECES
     ways = ((0, right), (1, left))
 
     loads = [
@@ -73,11 +75,12 @@
     rows[0, :count, width:] = packed.astype(jnp.bfloat16)
     sums[0] = jnp.zeros((count, width), jnp.bfloat16)
 
-    def token_copy(step, way, target):
-        part = pl.ds(way * half, half)
+    def token_copy(step, way, piece, target):
+        size = chunk if piece < PIECES - 1 else chunk + LANES
+        part = (pl.ds(way * half, half), pl.ds(piece * chunk, size))
         return pltpu.make_async_remote_copy(
-            src_ref=rows.at[step, part], dst_ref=rows.at[step + 1, part],
-            send_sem=tok_send.at[step, way], recv_sem=tok_recv.at[step + 1, way],
+            src_ref=rows.at[step, *part], dst_ref=rows.at[step + 1, *part],
+            send_sem=tok_send.at[step, way, piece], recv_sem=tok_recv.at[step + 1, way, piece],
             device_id=target, device_id_type=MESH,
         )
 
@@ -95,121 +98,154 @@
             device_id=twin, device_id_type=MESH,
         )
 
-    def sum_copy(step, way, target):
-        part = pl.ds(way * half, half)
+    def sum_copy(step, way, piece, target):
+        part = (pl.ds(way * half, half), pl.ds(piece * chunk, chunk))
         return pltpu.make_async_remote_copy(
-            src_ref=sums.at[step - 1, part], dst_ref=sums.at[step, part],
-            send_sem=sum_send.at[step - 1, way], recv_sem=sum_recv.at[step, way],
+            src_ref=sums.at[step - 1, *part], dst_ref=sums.at[step, *part],
+            send_sem=sum_send.at[step - 1, way, piece], recv_sem=sum_recv.at[step, way, piece],
             device_id=target, device_id_type=MESH,
         )
 
     def pass_on(step):
-        @pl.when(step > 0)
-        def _():
-            for way, target in ways:
-                token_copy(step - 1, way, target).wait_recv()
-
-        @pl.when(step < chips - 1)
-        def _():
-            for way, target in ways:
-                token_copy(step, way, target).start()
+        for piece in range(PIECES):
+            @pl.when(step > 0)
+            def _():
+                for way, target in ways:
+                    token_copy(step - 1, way, piece, target).wait_recv()
+
+            @pl.when(step < chips - 1)
+            def _():
+                for way, target in ways:
+                    token_copy(step, way, piece, target).start()
 
         swap_copy(step).start()
 
-    def ffn(step):
+    def up_phase(pair):
         def up_tile(tile, carry):
             columns = pl.ds(pl.multiple_of(tile * TILE, TILE), TILE)
-            block = rows[step, :, :width]
+            block = rows[pl.ds(2 * pair, 2), :, :width].reshape(4 * count, width)
             gate = jnp.dot(block, wg[:, columns], preferred_element_type=jnp.float32)
             up = jnp.dot(block, wu[:, columns], preferred_element_type=jnp.float32)
             hidden[:, columns] = (gate / (1.0 + jnp.exp(-gate)) * up).astype(jnp.bfloat16)
             return carry
 
         lax.fori_loop(0, hidden.shape[1] // TILE, up_tile, 0)
-        lane = lax.broadcasted_iota(jnp.int32, (2 * count, LANES), 1)
-        packed = rows[step, :, width:].astype(jnp.float32)
+
+    def down_phase(pair):
+        lane = lax.broadcasted_iota(jnp.int32, (4 * count, LANES), 1)
+        packed = rows[pl.ds(2 * pair, 2), :, width:].reshape(4 * count, LANES).astype(jnp.float32)
         share = jnp.sum(jnp.where(lane % experts == me, packed, 0.0), axis=1, keepdims=True)
 
         def down_tile(tile, carry):
             columns = pl.ds(pl.multiple_of(tile * TILE, TILE), TILE)
             result = jnp.dot(hidden[...], wd[:, columns], preferred_element_type=jnp.float32) * share
-            own[:, columns] = result[:count]
-            part_out[step % 2, :, columns] = result[count:].astype(jnp.bfloat16)
+            for turn in range(2):
+                at = 2 * turn * count
+                own[turn, :, columns] = result[at:at + count]
+                part_out[turn, :, columns] = result[at + count:at + 2 * count].astype(jnp.bfloat16)
             return carry
 
         lax.fori_loop(0, tiles, down_tile, 0)
 
     pl.semaphore_wait(barrier, 3)
     pass_on(0)
-    swap_copy(0).wait_recv()
-    for load in loads:
-        load.wait()
-    ffn(0)
-    part_copy(0).start()
     pass_on(1)
-    part_copy(0).wait_recv()
-
-    def keep_tile(tile, carry):
-        columns = pl.ds(pl.multiple_of(tile * TILE, TILE), TILE)
-        first[:, columns] = own[:, columns] + part_in[0, :, columns].astype(jnp.float32)
-        return carry
-
-    lax.fori_loop(0, tiles, keep_tile, 0)
+    loads[0].wait()
+    loads[1].wait()
+
+    def keep_first():
+        part_copy(0).wait_recv()
+
+        def keep_tile(tile, carry):
+            columns = pl.ds(pl.multiple_of(tile * TILE, TILE), TILE)
+            first[:, columns] = own[0, :, columns] + part_in[0, :, columns].astype(jnp.float32)
+            return carry
+
+        lax.fori_loop(0, tiles, keep_tile, 0)
 
     def send_sums(step):
         part_copy(step).wait_recv()
 
-        @pl.when(step > 1)
-        def _():
+        for piece in range(PIECES):
+            @pl.when(step > 1)
+            def _():
+                for way, target in ways:
+                    sum_copy(step - 1, way, piece, target).wait_recv()
+
+            def add_tile(tile, carry):
+                columns = pl.ds(pl.multiple_of(piece * chunk + tile * TILE, TILE), TILE)
+                total = own[step % 2, :, columns] + part_in[step, :, columns].astype(jnp.float32)
+                total = total + sums[step - 1, :, columns].astype(jnp.float32)
+                sums[step - 1, :, columns] = total.astype(jnp.bfloat16)
+                return carry
+
+            lax.fori_loop(0, chunk // TILE, add_tile, 0)
             for way, target in ways:
-                sum_copy(step - 1, way, target).wait_recv()
-
-        def add_tile(tile, carry):
-            columns = pl.ds(pl.multiple_of(tile * TILE, TILE), TILE)
-            total = own[:, columns] + part_in[step, :, columns].astype(jnp.float32)
-            total = total + sums[step - 1, :, columns].astype(jnp.float32)
-            sums[step - 1, :, columns] = total.astype(jnp.bfloat16)
+                sum_copy(step, way, piece, target).start()
+
+    def turn(pair, carry):
+        swap_copy(2 * pair).wait_recv()
+        swap_copy(2 * pair + 1).wait_recv()
+        up_phase(pair)
+
+        @pl.when(2 * pair + 2 < chips)
+        def _():
+            pass_on(2 * pair + 2)
+
+        @pl.when(pair == 0)
+        def _():
+            loads[2].wait()
+
+        @pl.when(pair > 1)
+        def _():
+            send_sums(2 * pair - 1)
+
+        @pl.when(pair > 0)
+        def _():
+            part_copy(2 * pair - 2).wait_send()
+            part_copy(2 * pair - 1).wait_send()
+
+        down_phase(pair)
+        part_copy(2 * pair).start()
+        part_copy(2 * pair + 1).start()
+
+        @pl.when(2 * pair + 3 < chips)
+        def _():
+            pass_on(2 * pair + 3)
+
+        @pl.when(pair == 0)
+        def _():
+            send_sums(1)
+            keep_first()
+
+        @pl.when(pair > 0)
+        def _():
+            send_sums(2 * pair)
+
+        return carry
+
+    lax.fori_loop(0, chips // 2, turn, 0)
+    send_sums(chips - 1)
+    for piece in range(PIECES):
+        for way, target in ways:
+            sum_copy(chips - 1, way, piece, target).wait_recv()
+
+        def last_tile(tile, carry):
+            columns = pl.ds(pl.multiple_of(piece * chunk + tile * TILE, TILE), TILE)
+            total = first[:, columns] + sums[chips - 1, :, columns].astype(jnp.float32)
+            out[:, columns] = total.astype(jnp.bfloat16)
             return carry
 
-        lax.fori_loop(0, tiles, add_tile, 0)
-        for way, target in ways:
-            sum_copy(step, way, target).start()
-
-    def turn(step, carry):
-        swap_copy(step).wait_recv()
-
-        @pl.when(step > 1)
-        def _():
-            part_copy(step - 2).wait_send()
-
-        ffn(step)
-        part_copy(step).start()
-
-        @pl.when(step < chips - 1)
-        def _():
-            pass_on(step + 1)
-
-        send_sums(step)
-        return carry
-
-    lax.fori_loop(1, chips, turn, 0)
-    for way, target in ways:
-        sum_copy(chips - 1, way, target).wait_recv()
-
-    def last_tile(tile, carry):
-        columns = pl.ds(pl.multiple_of(tile * TILE, TILE), TILE)
-        total = first[:, columns] + sums[chips - 1, :, columns].astype(jnp.float32)
-        out[:, columns] = total.astype(jnp.bfloat16)
-        return carry
-
-    lax.fori_loop(0, tiles, last_tile, 0)
+        lax.fori_loop(0, chunk // TILE, last_tile, 0)
+
     part_copy(chips - 1).wait_send()
     part_copy(chips - 2).wait_send()
 
     def drain(step, carry):
         for way, target in ways:
-            token_copy(step, way, target).wait_send()
-            sum_copy(step + 1, way, target).wait_send()
+            for piece in range(PIECES):
+                token_copy(step, way, piece, target).wait_send()
+                sum_copy(step + 1, way, piece, target).wait_send()
         return carry
 
     lax.fori_loop(0, chips - 1, drain, 0)
@@ -240,17 +276,17 @@
             pltpu.VMEM((width, ff), jnp.bfloat16),
             pltpu.VMEM((ff, width), jnp.bfloat16),
             pltpu.VMEM((chips, 2 * count, width + LANES), jnp.bfloat16),
-            pltpu.VMEM((2 * count, ff), jnp.bfloat16),
-            pltpu.VMEM((count, width), jnp.float32),
+            pltpu.VMEM((4 * count, ff), jnp.bfloat16),
+            pltpu.VMEM((2, count, width), jnp.float32),
             pltpu.VMEM((count, width), jnp.float32),
             pltpu.VMEM((2, count, width), jnp.bfloat16),
             pltpu.VMEM((chips, count, width), jnp.bfloat16),
             pltpu.VMEM((chips, count, width), jnp.bfloat16),
             dma((3,)),
-            dma((chips, 2)), dma((chips, 2)),
+            dma((chips, 2, PIECES)), dma((chips, 2, PIECES)),
             dma((chips,)), dma((chips,)),
             dma((chips,)), dma((chips,)),
-            dma((chips, 2)), dma((chips, 2)),
+            dma((chips, 2, PIECES)), dma((chips, 2, PIECES)),
         ],
         cost_estimate=pl.CostEstimate(
             flops=flops, bytes_accessed=6 * width * ff, transcendentals=2 * chips * count * ff

time: 102 us -> 92.3 us (0.905)
  Pallas kernels: 95.3 us -> 86.1 us
    pallas_call x1, Pallas kernels: 95.3 us -> 86.1 us  [body(): pl.pallas_call(functools.partial(kernel, chips, experts), out_shape=jax.S...]
where the time goes in v3:
time: 92.3 us; the launch traced here: 92 us
  Pallas kernels  86.1 us (93%)
  local copies, waits for them, and re-layouts  5.95 us (6%)
    pallas_call x1, Pallas kernels, body(): pl.pallas_call(functools.partial(kernel, chips, experts), out_shape=jax.S...  86.1 us
    unnamed x4, local copies, waits for them, and re-layouts  5.95 us

profile of v3, /device:TPU:0, one launch (start us, length us, event | category | flops | bytes accessed | tf_op | source)
XLA Modules:
  0.0 92.0 jit_solution(5084217410208394384)
XLA Ops:
  0.0 1.4 %copy.8.scales = bf16[64,28]{1,0:T(8,128)(2,1)} copy(bf16[64,28]{0,1:T(8,128)(2,1)} %param.8) | data formatting | bytes 7168 | tf_op args[1]
  1.4 1.4 %copy.9.ids = s32[64,8]{1,0:T(8,128)} copy(s32[64,8]{0,1:T(8,128)} %param.9) | data formatting | bytes 4096 | tf_op args[2]
  2.8 1.4 %copy.10.weights = f32[64,8]{1,0:T(8,128)} copy(f32[64,8]{0,1:T(8,128)} %param.10) | data formatting | bytes 4096 | tf_op args[3]
  4.1 86.1 %shard_map.73 = bf16[64,3584]{1,0:T(8,128)(2,1)} custom-call(bf16[64,3584]{1,0:T(8,128)(2,1)} %tokens.1, bf16[64,28]{1,0:T(8,128)(2,1)} %copy.8.scales, s32[64,8]{1,0:T(8,128)} %copy.9.ids, f32[64,8]{1,0:T(8,128)} %copy.10.weights, bf16[1,3584,1024]{2,1,0:T(8,128)(2,1)} %gate_hbm.1, bf16[1,3584,1024]{2,1,0:T(8,128)(2,1)} %up_hbm.1, ...), custom_call_target="tpu_custom_call" | custom-call | flops 22548578304 | bytes 22020096 | tf_op jit(solution)/shard_map/pallas_call | solution.py:269
  90.2 1.8 %copy.12 = bf16[64,3584]{1,0:T(8,128)(2,1)} copy(bf16[64,3584]{1,0:T(8,128)(2,1)} %shard_map.73) | data formatting | bytes 917504

commit v4 on v3

--- a/solution.py
+++ b/solution.py
@@ -59,20 +59,29 @@
     for other in (right, left, twin):
         pl.semaphore_signal(barrier, inc=1, device_id=other, device_id_type=MESH)
 
+    def upright(flat):
+        size = flat.shape[0]
+        same = lax.broadcasted_iota(jnp.int32, (size, size), 0) == lax.broadcasted_iota(jnp.int32, (size, size), 1)
+        return lax.dot_general(
+            flat, same.astype(jnp.float32).astype(jnp.bfloat16), (((0,), (0,)), ((), ())),
+            preferred_element_type=jnp.float32,
+        )
+
+    factors = upright(scales[...])
     for block in range(width // LANES):
         columns = slice(block * LANES, (block + 1) * LANES)
-        scaled = tokens[:, columns].astype(jnp.float32) * scales[:, block:block + 1].astype(jnp.float32)
+        scaled = tokens[:, columns].astype(jnp.float32) * factors[:, block:block + 1]
         rows[0, :count, columns] = scaled.astype(jnp.bfloat16)
-    lane = lax.broadcasted_iota(jnp.int32, (count, LANES), 1)
-    dense = jnp.zeros((count, LANES), jnp.float32)
-    for route in range(ids.shape[1]):
-        dense = dense + jnp.where(ids[:, route:route + 1] == lane % experts, weights[:, route:route + 1], 0.0)
+    line = lax.broadcasted_iota(jnp.int32, (LANES, count), 0)
+    dense = jnp.zeros((LANES, count), jnp.float32)
+    for route in range(ids.shape[0]):
+        dense = dense + jnp.where(ids[route:route + 1, :] == line % experts, weights[route:route + 1, :], 0.0)
     high = dense.astype(jnp.bfloat16).astype(jnp.float32)
     middle = (dense - high).astype(jnp.bfloat16).astype(jnp.float32)
     low = dense - high - middle
-    piece = lane // experts
+    piece = line // experts
     packed = jnp.where(piece == 0, high, jnp.where(piece == 1, middle, jnp.where(piece == 2, low, 0.0)))
-    rows[0, :count, width:] = packed.astype(jnp.bfloat16)
+    rows[0, :count, width:] = upright(packed.astype(jnp.bfloat16)).astype(jnp.bfloat16)
     sums[0] = jnp.zeros((count, width), jnp.bfloat16)
 
     def token_copy(step, way, piece, target):
@@ -294,7 +303,7 @@
         compiler_params=pltpu.CompilerParams(
             collective_id=0, has_side_effects=True, vmem_limit_bytes=60 * 1024 * 1024
         ),
-    )(tokens, scales, expert_ids, route_weights, w_gate, w_up, w_down)
+    )(tokens, scales.T, expert_ids.T, route_weights.T, w_gate, w_up, w_down)
 
 
 def solution(mesh):

time: 92.3 us -> 88.1 us (0.954)
  local copies, waits for them, and re-layouts: 5.95 us -> 1.82 us
    unnamed x4 -> x1, local copies, waits for them, and re-layouts: 5.95 us -> 1.82 us
where the time goes in v4:
time: 88.1 us; the launch traced here: 87.9 us
  Pallas kernels  86.1 us (98%)
  local copies, waits for them, and re-layouts  1.82 us (2%)
    pallas_call x1, Pallas kernels, body(): pl.pallas_call(functools.partial(kernel, chips, experts), out_shape=jax.S...  86.1 us
    unnamed x1, local copies, waits for them, and re-layouts  1.82 us

profile of v4, /device:TPU:0, one launch (start us, length us, event | category | flops | bytes accessed | tf_op | source)
XLA Modules:
  0.0 87.9 jit_solution(1236582059181480724)
XLA Ops:
  0.0 86.1 %shard_map.73 = bf16[64,3584]{1,0:T(8,128)(2,1)} custom-call(bf16[64,3584]{1,0:T(8,128)(2,1)} %tokens.1, bf16[28,64]{1,0:T(8,128)(2,1)} %bitcast.3, s32[8,64]{1,0:T(8,128)} %bitcast.4, f32[8,64]{1,0:T(8,128)} %bitcast.5, bf16[1,3584,1024]{2,1,0:T(8,128)(2,1)} %gate_hbm.1, bf16[1,3584,1024]{2,1,0:T(8,128)(2,1)} %up_hbm.1, bf16[1,1024,3584]{2,1,0:T(8,128)(2,1)} %down_hbm.1), custom_call_target="tpu_custom_call" | custom-call | flops 22548578304 | bytes 22020096 | tf_op jit(solution)/shard_map/pallas_call | solution.py:278
  86.1 1.8 %copy.9 = bf16[64,3584]{1,0:T(8,128)(2,1)} copy(bf16[64,3584]{1,0:T(8,128)(2,1)} %shard_map.73) | data formatting | bytes 917504

commit v5 on v4

--- a/solution.py
+++ b/solution.py
@@ -100,10 +100,11 @@
             device_id=twin, device_id_type=MESH,
         )
 
-    def part_copy(step):
+    def part_copy(step, piece):
+        columns = pl.ds(piece * chunk, chunk)
         return pltpu.make_async_remote_copy(
-            src_ref=part_out.at[step % 2], dst_ref=part_in.at[step],
-            send_sem=part_send.at[step], recv_sem=part_recv.at[step],
+            src_ref=part_out.at[step % 2, :, columns], dst_ref=part_in.at[step, :, columns],
+            send_sem=part_send.at[step, piece], recv_sem=part_recv.at[step, piece],
             device_id=twin, device_id_type=MESH,
         )
 
@@ -154,7 +155,14 @@
                 part_out[turn, :, columns] = result[at + count:at + 2 * count].astype(jnp.bfloat16)
             return carry
 
-        lax.fori_loop(0, tiles, down_tile, 0)
+        for piece in range(PIECES):
+            lax.fori_loop(piece * chunk // TILE, (piece + 1) * chunk // TILE, down_tile, 0)
+            part_copy(2 * pair, piece).start()
+            part_copy(2 * pair + 1, piece).start()
+            if piece == 0:
+                @pl.when(jnp.logical_and(pair > 0, 2 * pair + 3 < chips))
+                def _():
+                    pass_on(2 * pair + 3)
 
     pl.semaphore_wait(barrier, 3)
     pass_on(0)
@@ -163,7 +171,8 @@
     loads[1].wait()
 
     def keep_first():
-        part_copy(0).wait_recv()
+        for piece in range(PIECES):
+            part_copy(0, piece).wait_recv()
 
         def keep_tile(tile, carry):
             columns = pl.ds(pl.multiple_of(tile * TILE, TILE), TILE)
@@ -173,9 +182,9 @@
         lax.fori_loop(0, tiles, keep_tile, 0)
 
     def send_sums(step):
-        part_copy(step).wait_recv()
-
         for piece in range(PIECES):
+            part_copy(step, piece).wait_recv()
+
             @pl.when(step > 1)
             def _():
                 for way, target in ways:
@@ -211,19 +220,14 @@
 
         @pl.when(pair > 0)
         def _():
-            part_copy(2 * pair - 2).wait_send()
-            part_copy(2 * pair - 1).wait_send()
+            for piece in range(PIECES):
+                part_copy(2 * pair - 2, piece).wait_send()
+                part_copy(2 * pair - 1, piece).wait_send()
 
         down_phase(pair)
-        part_copy(2 * pair).start()
-        part_copy(2 * pair + 1).start()
-
-        @pl.when(2 * pair + 3 < chips)
-        def _():
-            pass_on(2 * pair + 3)
-
         @pl.when(pair == 0)
         def _():
+            pass_on(3)
             send_sums(1)
             keep_first()
 
@@ -247,8 +251,9 @@
 
         lax.fori_loop(0, chunk // TILE, last_tile, 0)
 
-    part_copy(chips - 1).wait_send()
-    part_copy(chips - 2).wait_send()
+    for piece in range(PIECES):
+        part_copy(chips - 1, piece).wait_send()
+        part_copy(chips - 2, piece).wait_send()
 
     def drain(step, carry):
         for way, target in ways:
@@ -294,7 +299,7 @@
             dma((3,)),
             dma((chips, 2, PIECES)), dma((chips, 2, PIECES)),
             dma((chips,)), dma((chips,)),
-            dma((chips,)), dma((chips,)),
+            dma((chips, PIECES)), dma((chips, PIECES)),
             dma((chips, 2, PIECES)), dma((chips, 2, PIECES)),
         ],
         cost_estimate=pl.CostEstimate(

time: 88.1 us -> 87.3 us (level)
  no operation moved by 1% of the time
where the time goes in v5:
time: 87.3 us; the launch traced here: 87.1 us
  Pallas kernels  85.3 us (98%)
  local copies, waits for them, and re-layouts  1.82 us (2%)
    pallas_call x1, Pallas kernels, body(): pl.pallas_call(functools.partial(kernel, chips, experts), out_shape=jax.S...  85.3 us
    unnamed x1, local copies, waits for them, and re-layouts  1.82 us

profile of v5, /device:TPU:0, one launch (start us, length us, event | category | flops | bytes accessed | tf_op | source)
XLA Modules:
  0.0 87.1 jit_solution(6022748657097654012)
XLA Ops:
  0.0 85.3 %shard_map.73 = bf16[64,3584]{1,0:T(8,128)(2,1)} custom-call(bf16[64,3584]{1,0:T(8,128)(2,1)} %tokens.1, bf16[28,64]{1,0:T(8,128)(2,1)} %bitcast.3, s32[8,64]{1,0:T(8,128)} %bitcast.4, f32[8,64]{1,0:T(8,128)} %bitcast.5, bf16[1,3584,1024]{2,1,0:T(8,128)(2,1)} %gate_hbm.1, bf16[1,3584,1024]{2,1,0:T(8,128)(2,1)} %up_hbm.1, bf16[1,1024,3584]{2,1,0:T(8,128)(2,1)} %down_hbm.1), custom_call_target="tpu_custom_call" | custom-call | flops 22548578304 | bytes 22020096 | tf_op jit(solution)/shard_map/pallas_call | solution.py:283
  85.3 1.8 %copy.9 = bf16[64,3584]{1,0:T(8,128)(2,1)} copy(bf16[64,3584]{1,0:T(8,128)(2,1)} %shard_map.73) | data formatting | bytes 917504
